TPU v7x, 32 devices: a whole 2x2x4 slice. The times are simulated.
32 devices in a mesh: grp: 2 (over y), tblk: 4 (over x, core), inp: 4 (over z).
Axes of the slice: x: 2, y: 2, z: 4, core: 2. Of those that a mesh axis runs over, the one named last changes fastest.
Arguments:
- volt: bfloat16 [2, 192, 2, 512, 1024], P(None, 'grp', None, 'inp', 'tblk'), parts along dimension 1, may hold values from -20 to 20
- gains: float32 [2, 192, 512], P(None, ('grp', 'inp')), parts along dimension 1, may hold values from -0.25 to 0.25
- positions: float32 [3, 512], replicated, may hold values from -4 to 4
- directions: float32 [3, 256], replicated, may hold values from -1 to 1
- pattern: int32 [32, 64], replicated, may hold values 0 or 1
- dm_bins: int32 [256], replicated, may hold values from 0 to 31
- retention: float32 [256, 1024], P(None, 'tblk'), may hold values from 0.5 to 1
Outputs:
- detected: float32 [256, 192, 1024], P(None, ('grp', 'inp'), 'tblk'), parts along dimension 1
There are 2 independent parts, one for each index of `grp`. A program takes and returns all parts, laid end to end along the dimension named above; an argument that names none is the same for every part. Nothing has to cross between parts.
All inputs are finite; a program needn't handle non-finite values.
Results may differ from a plain program's by a relative error of at most 0.0076.
Values may be sent and summed in bfloat16 or wider, within the bound.
A program may use at most 256 MiB of HBM per device.

v0:
```python
import math

import jax
import jax.numpy as jnp
from jax import lax
from jax.sharding import PartitionSpec as P

C = 96
NDM = 32


def from_behind(x, axis, by):
    devices = lax.axis_size(axis)
    pairs = [(i, i + by) for i in range(devices) if 0 <= i + by < devices]
    return lax.ppermute(x, axis, pairs)


def carried_in(value, axis, join, neutral):
    count, mine = (lax.axis_size(axis), lax.axis_index(axis))
    pieces = jax.tree.map(lambda part: lax.all_gather(part, axis), value)
    total = jax.tree.map(
        lambda part, zero: jnp.full_like(part, 0) + jnp.asarray(zero, part.dtype), value, neutral
    )

    def lap(position, total):
        longer = join(total, jax.tree.map(lambda part: part[position], pieces))
        return jax.tree.map(lambda new, old: jnp.where(position < mine, new, old), longer, total)

    return lax.fori_loop(0, count - 1, lap, total)


def beam_weights(gains, positions, directions, pattern, frequency):
    delay = (
        directions[0][:, None] * positions[0][None, :]
        + directions[1][:, None] * positions[1][None, :]
        + directions[2][:, None] * positions[2][None, :]
    )
    turning = 2.0 * math.pi * frequency
    phase = turning[:, None, None] * delay[None, :, :]
    blocked = jnp.repeat(jnp.repeat(pattern, 8, axis=0), 8, axis=1).astype(jnp.float32)
    cosine = jnp.cos(phase)
    sine = jnp.sin(phase)
    real_part = blocked[None] * (gains[0][:, None, :] * cosine + gains[1][:, None, :] * sine)
    imag_part = blocked[None] * (gains[1][:, None, :] * cosine - gains[0][:, None, :] * sine)
    upper = jnp.concatenate([real_part, -imag_part], axis=-1)
    lower = jnp.concatenate([imag_part, real_part], axis=-1)
    return jnp.stack([upper, lower], axis=2).astype(jnp.bfloat16)


def transform_tables(length):
    extent = 2 * length
    indices = jnp.arange(extent, dtype=jnp.int32)
    product = indices[:, None] * indices[None, :] % extent
    angle = product.astype(jnp.float32) * (math.pi / length)
    cosine = jnp.cos(angle).astype(jnp.bfloat16)
    sine = jnp.sin(angle).astype(jnp.bfloat16)
    forward = jnp.concatenate(
        [jnp.concatenate([cosine, -sine], axis=1), jnp.concatenate([sine, cosine], axis=1)], axis=0
    )
    inverse = jnp.concatenate(
        [
            jnp.concatenate([cosine[:, length:], sine[:, length:]], axis=1),
            jnp.concatenate([-sine[:, length:], cosine[:, length:]], axis=1),
        ],
        axis=0,
    )
    forward_prev = jnp.concatenate([forward[:length], forward[2 * length : 3 * length]], axis=0)
    forward_cur = jnp.concatenate([forward[length : 2 * length], forward[3 * length :]], axis=0)
    return (forward_prev, forward_cur, inverse[:extent], inverse[extent:])


def chirp_factors(dm_bins, frequency, length, bins_total):
    extent = 2 * length
    offsets = ((jnp.arange(extent, dtype=jnp.int32) + length) % extent - length).astype(
        jnp.float32
    ) / extent
    measure = (dm_bins + 1).astype(jnp.float32) / bins_total
    angle = (
        (math.pi * length * measure)[None, :, None]
        * (offsets * offsets)[None, None, :]
        / (frequency * frequency * frequency)[:, None, None]
    )
    return (jnp.cos(angle), jnp.sin(angle))


def dedisperse(previous, current, tables, chirp_cos, chirp_sin):
    forward_prev, forward_cur, inverse_real, inverse_imag = tables
    channels_here, beams_count = (previous.shape[1], previous.shape[2])
    length = previous.shape[-1]
    extent = 2 * length
    power = jnp.zeros((channels_here * beams_count, length), jnp.float32)
    for polar in range(previous.shape[0]):
        rows_prev = previous[polar].reshape(-1, extent)
        rows_cur = current[polar].reshape(-1, extent)
        spectrum = jnp.dot(rows_prev, forward_prev, preferred_element_type=jnp.float32) + jnp.dot(
            rows_cur, forward_cur, preferred_element_type=jnp.float32
        )
        real_part = spectrum[:, :extent].reshape(channels_here, beams_count, extent)
        imag_part = spectrum[:, extent:].reshape(channels_here, beams_count, extent)
        turned_real = (
            (real_part * chirp_cos + imag_part * chirp_sin).reshape(-1, extent).astype(jnp.bfloat16)
        )
        turned_imag = (
            (imag_part * chirp_cos - real_part * chirp_sin).reshape(-1, extent).astype(jnp.bfloat16)
        )
        signal = (
            jnp.dot(turned_real, inverse_real, preferred_element_type=jnp.float32)
            + jnp.dot(turned_imag, inverse_imag, preferred_element_type=jnp.float32)
        ) * (1.0 / extent)
        power = (
            power
            + signal[:, :length] * signal[:, :length]
            + signal[:, length:] * signal[:, length:]
        )
    return power.reshape(channels_here, beams_count, length)


def combine_maps(earlier, later):
    return (
        later[0] * earlier[0],
        later[0] * earlier[1] + later[1],
        later[0] * earlier[2] + later[2],
    )


def running_level(power, retention):
    channels_here, beams_count, length = power.shape
    log_keep = jnp.cumsum(jnp.log(retention), axis=1)
    renewal = 1.0 - retention
    beam_block = math.gcd(beams_count, 32)
    block_count = beams_count // beam_block
    lower_mask = (
        jnp.arange(length, dtype=jnp.int32)[:, None] >= jnp.arange(length, dtype=jnp.int32)[None, :]
    )

    def level_block(index):
        start = index * beam_block
        cum_part = lax.dynamic_slice_in_dim(log_keep, start, beam_block, 0)
        renew_part = lax.dynamic_slice_in_dim(renewal, start, beam_block, 0)
        power_part = lax.dynamic_slice_in_dim(power, start, beam_block, 1)
        spread = cum_part[:, :, None] - cum_part[:, None, :]
        kernel = (
            jnp.where(lower_mask[None], jnp.exp(jnp.where(lower_mask[None], spread, 0.0)), 0.0)
            * renew_part[:, None, :]
        )
        return jnp.einsum("cbu,btu->cbt", power_part, kernel, precision=lax.Precision.HIGHEST)

    levels = lax.map(level_block, jnp.arange(block_count, dtype=jnp.int32))
    run_level = jnp.moveaxis(levels, 0, 1).reshape(channels_here, beams_count, length)
    return (jnp.exp(log_keep), run_level, -jnp.expm1(log_keep))


def per_device(volt, gains, positions, directions, pattern, dm_bins, retention):
    channels_here = gains.shape[1]
    length = volt.shape[-1]
    channel_ids = lax.axis_index("inp") * channels_here + jnp.arange(channels_here, dtype=jnp.int32)
    frequency = 1.0 + channel_ids.astype(jnp.float32) / C
    station_weights = beam_weights(gains, positions, directions, pattern, frequency)
    samples = lax.all_to_all(volt, "inp", split_axis=1, concat_axis=3, tiled=True)
    formed = []
    for polar in range(samples.shape[0]):
        flattened = samples[polar].reshape(channels_here, -1, length)
        formed.append(
            jnp.einsum(
                "cbrs,csl->cbrl", station_weights, flattened, preferred_element_type=jnp.float32
            ).astype(jnp.bfloat16)
        )
    exchanged = jnp.stack(formed, axis=0)
    previous_beams = from_behind(exchanged, "tblk", 1)
    tables = transform_tables(length)
    chirp_cos, chirp_sin = chirp_factors(dm_bins, frequency, length, NDM)
    power = dedisperse(previous_beams, exchanged, tables, chirp_cos, chirp_sin)
    run_decay, run_level, run_weight = running_level(power, retention)
    state_shape = power.shape[:2]
    total_decay = jnp.broadcast_to(run_decay[None, :, -1], state_shape)
    total_level = run_level[:, :, -1]
    weight_total = jnp.broadcast_to(run_weight[None, :, -1], state_shape)
    identity = (
        jnp.ones(state_shape, jnp.float32),
        jnp.zeros(state_shape, jnp.float32),
        jnp.zeros(state_shape, jnp.float32),
    )
    carried = carried_in((total_decay, total_level, weight_total), "tblk", combine_maps, identity)
    entry_level = carried[1]
    entry_weight = carried[2]
    level_full = run_decay[None] * entry_level[:, :, None] + run_level
    weight_full = run_decay[None] * entry_weight[:, :, None] + run_weight[None]
    return jnp.transpose(power - level_full / weight_full, (1, 0, 2))


def solution(mesh):
    placed = (
        P(None, "grp", None, "inp", "tblk"),
        P(None, ("grp", "inp"), None),
        P(),
        P(),
        P(),
        P(),
        P(None, "tblk"),
    )
    return jax.shard_map(
        per_device,
        mesh=mesh,
        in_specs=placed,
        out_specs=P(None, ("grp", "inp"), "tblk"),
        check_vma=False,
    )
```

profile of v0, /device:TPU:0, one launch (start us, length us, event | category | flops | bytes accessed | tf_op | source)
XLA Modules:
  0.0 1158.6 jit_solution(13220483020951914972)
XLA Ops:
  0.0 20.8 %copy.50 = bf16[2,96,2,128,256]{4,3,2,0,1:T(8,128)(2,1)} copy(bf16[2,96,2,128,256]{4,3,2,1,0:T(8,128)(2,1)} %param.11) | data formatting | bytes 50331648 | tf_op args[0]
  20.8 8.5 all-to-all-start
  30.0 48.9 %fusion.33 = (bf16[24,256,512]{2,1,0:T(8,128)(2,1)S(1)}, bf16[24,256,512]{2,1,0:T(8,128)(2,1)S(1)}, bf16[24,256,512]{2,1,0:T(8,128)(2,1)S(1)}) fusion(f32[24,512]{1,0:T(8,128)S(1)} %get-tuple-element.314, f32[256,512]{1,0:T(8,128)S(1)} %multiply_add_fusion, f32[24]{0:T(128)S(1)} %get-tuple-element.322, f32[24,512]{1,0:T(8,128)S(1)} %get-tuple-element.313, ...), kind=kLoop, calls=%fused_computation.43 | loop fusion | flops 40894464 | bytes 20021344 | tf_op jit(solution)/shard_map/convert.7
  79.0 9.5 maximum_bitcast_fusion
  88.4 485.2 %all-to-all-done = bf16[2,96,2,128,256]{4,3,2,0,1:T(8,128)(2,1)} async-done(((bf16[2,96,2,128,256]{4,3,2,0,1:T(8,128)(2,1)}), bf16[2,96,2,128,256]{4,3,2,0,1:T(8,128)(2,1)}, u32[]{:S(2)}, u32[]{:S(2)}) %all-to-all-start) | async-done | bytes 25165856 | tf_op jit(solution)/shard_map/all_to_all | solution.py:159
  573.6 12.2 %copy.82 = bf16[2,4,24,2,128,256]{5,4,1,3,2,0:T(8,128)(2,1)S(1)} copy(bf16[2,4,24,2,128,256]{5,4,3,0,2,1:T(8,128)(2,1)} %bitcast.13) | data formatting | bytes 50331648 | tf_op jit(solution)/shard_map/all_to_all | solution.py:159
  585.9 8.9 fusion.73
  594.7 18.8 %fusion.39 = bf16[24,256,2,256]{3,1,2,0:T(8,128)(2,1)} fusion(bf16[24,1024,256,1]{2,1,3,0:T(8,128)(2,1)} %bitcast.151, bf16[24,256,1,1024]{3,1,2,0:T(8,128)(2,1)} %get-tuple-element.299, bf16[24,256,1,1024]{3,1,2,0:T(8,128)(2,1)} %get-tuple-element.298), kind=kOutput, calls=%fused_computation.66 | convolution fusion | flops 6458179584 | bytes 44040192 | tf_op jit(solution)/shard_map/cbrs,csl->cbrl/dot_general | solution.py:164
  613.6 19.3 %fusion.40 = bf16[24,256,2,256]{3,1,2,0:T(8,128)(2,1)} fusion(bf16[24,1024,256,1]{2,1,3,0:T(8,128)(2,1)} %bitcast.150, bf16[24,256,1,1024]{3,1,2,0:T(8,128)(2,1)} %get-tuple-element.299, bf16[24,256,1,1024]{3,1,2,0:T(8,128)(2,1)} %get-tuple-element.298), kind=kOutput, calls=%fused_computation.67 | convolution fusion | flops 6458179584 | bytes 44040192 | tf_op jit(solution)/shard_map/cbrs,csl->cbrl/dot_general | solution.py:164
  632.9 10.5 pad_maximum_fusion.3
  666.3 124.5 %all-gather.2 = f32[1024,1]{0,1:T(1,128)S(1)} all-gather(f32[256,1]{0,1:T(1,128)S(1)} %slice.169), channel_id=6, replica_groups=mesh['grp'=2,'tblk'=4,'inp'=4] {'tblk'}, dimensions={0}, use_global_device_ids=true | all-gather | bytes 5120 | tf_op jit(solution)/shard_map/all_gather | solution.py:20
  797.2 9.1 copy.55
  806.3 9.1 copy.53
  827.9 10.4 fusion.74
  838.2 9.2 copy.54
  855.0 9.2 copy.52
  869.3 12.0 %fusion.51 = f32[6144,1024]{1,0:T(8,128)} fusion(bf16[6144,512]{0,1:T(8,128)(2,1)S(1)} %bitcast.154, bf16[256,1024]{1,0:T(8,128)(2,1)S(1)} %copy-done.3, bf16[256,1024]{1,0:T(8,128)(2,1)S(1)} %get-tuple-element.307), kind=kOutput, calls=%fused_computation.90 | convolution fusion | flops 6444548096 | bytes 32505856 | tf_op jit(solution)/shard_map/dot_general | solution.py:95
  881.3 11.8 %fusion.52 = f32[6144,1024]{1,0:T(8,128)} fusion(bf16[6144,512]{0,1:T(8,128)(2,1)S(1)} %bitcast.155, bf16[256,1024]{1,0:T(8,128)(2,1)S(1)} %copy-done.3, bf16[256,1024]{1,0:T(8,128)(2,1)S(1)} %get-tuple-element.307), kind=kOutput, calls=%fused_computation.91 | convolution fusion | flops 6444548096 | bytes 32505856 | tf_op jit(solution)/shard_map/dot_general | solution.py:95
  893.1 18.3 %convolution_add_fusion = f32[6144,1024]{1,0:T(8,128)} fusion(f32[6144,1024]{1,0:T(8,128)} %fusion.51, bf16[6144,512]{0,1:T(8,128)(2,1)} %bitcast.141, bf16[512,512]{1,0:T(8,128)(2,1)S(1)} %get-tuple-element.323, bf16[512,512]{1,0:T(8,128)(2,1)S(1)} %get-tuple-element.324, bf16[512,512]{1,0:T(8,128)(2,1)S(1)} %fusion.57), kind=kOutput, calls=%fused_computation.56 | convolution fusion | flops 6454509568 | bytes 58195968 | tf_op jit(solution)/shard_map/dot_general | solution.py:95
  911.4 18.5 %convolution_add_fusion.1 = f32[6144,1024]{1,0:T(8,128)} fusion(f32[6144,1024]{1,0:T(8,128)} %fusion.52, bf16[6144,512]{0,1:T(8,128)(2,1)} %bitcast.140, bf16[512,512]{1,0:T(8,128)(2,1)S(1)} %get-tuple-element.323, bf16[512,512]{1,0:T(8,128)(2,1)S(1)} %get-tuple-element.324, bf16[512,512]{1,0:T(8,128)(2,1)S(1)} %fusion.57), kind=kOutput, calls=%fused_computation.57 | convolution fusion | flops 6454509568 | bytes 58195968 | tf_op jit(solution)/shard_map/dot_general | solution.py:95
  929.9 56.9 %subtract_convert_fusion.1 = (bf16[6144,512]{1,0:T(8,128)(2,1)}, bf16[6144,512]{1,0:T(8,128)(2,1)S(1)}, bf16[6144,512]{1,0:T(8,128)(2,1)S(1)}, bf16[6144,512]{1,0:T(8,128)(2,1)S(1)}) fusion(f32[6144,1024]{1,0:T(8,128)} %convolution_add_fusion.1, f32[6144]{0:T(1024)S(1)} %bitcast.160, f32[256,512]{1,0:T(8,128)S(1)} %broadcast_multiply_fusion, ...), kind=kLoop, calls=%fused_computation.52 | loop fusion | flops 53477376 | bytes 76046336 | tf_op jit(solution)/shard_map/convert_element_type | solution.py:104
  996.6 11.2 add_multiply_fusion.1
  1014.5 11.9 %fusion.36 = f32[6144,256]{1,0:T(8,128)} fusion(f32[6144,512]{1,0:T(8,128)} %add_multiply_fusion, f32[6144,512]{1,0:T(8,128)} %add_multiply_fusion.1), kind=kLoop, calls=%fused_computation.59 | loop fusion | flops 11010048 | bytes 31457280 | tf_op jit(solution)/shard_map/add | solution.py:111
  1026.4 109.9 %while.28 = (s32[]{:T(128)}, f32[8,24,32,256]{3,2,0,1:T(8,128)}, s32[8]{0:T(128)S(1)}, f32[256,256]{1,0:T(8,128)}, f32[256,256]{1,0:T(8,128)}, /*index=5*/f32[24...) while((s32[]{:T(128)}, f32[8,24,32,256]{3,2,0,1:T(8,128)}, ...), condition=%wide.region_3.4_spmd.clone.clone, body=%wide.region_2.3_spmd.clone.clone.sunk | while | flops 612433920 | bytes 5046951 | solution.py:148
  1029.7 9.3 fusion.95
  1043.4 9.3 fusion.95
  1057.1 9.3 fusion.95
  1070.8 9.3 fusion.95
  1084.5 9.3 fusion.95
  1098.3 9.3 fusion.95
  1112.0 9.3 fusion.95
  1125.7 9.3 fusion.95
  (141 shorter events, 123.5 us)
Async XLA Ops:
  20.8 8.6 copy-start.8
  20.8 9.0 copy-start.10
  20.8 9.0 copy-start.9
  20.8 9.0 copy-start.5
  20.8 552.8 %all-to-all-start = ((bf16[2,96,2,128,256]{4,3,2,0,1:T(8,128)(2,1)}), bf16[2,96,2,128,256]{4,3,2,0,1:T(8,128)(2,1)}, u32[]{:S(2)}, u32[]{:S(2)}) async-start(bf16[2,96,2,128,256]{4,3,2,0,1:T(8,128)(2,1)} %copy.50), calls=%async_computation | async-start | bytes 50331648 | tf_op jit(solution)/shard_map/all_to_all | solution.py:159
  632.9 16.5 %copy-start.4 = (f32[256,256]{1,0:T(8,128)S(1)}, f32[256,256]{1,0:T(8,128)}, u32[]{:S(2)}) copy-start(f32[256,256]{1,0:T(8,128)} %param.17) | copy-start | bytes 786436
  643.4 153.7 %copy-start.11 = (s32[256]{0:T(256)S(1)}, s32[256]{0:T(256)}, u32[]{:S(2)}) copy-start(s32[256]{0:T(256)} %param.16) | copy-start | bytes 3076
  643.4 184.5 %collective-permute-start = (bf16[2,24,256,2,256]{4,2,3,1,0:T(8,128)(2,1)}, bf16[2,24,256,2,256]{4,2,3,1,0:T(8,128)(2,1)}, u32[]{:S(2)}, u32[]{:S(2)}) collective-permute-start(bf16[2,24,256,2,256]{4,2,3,1,0:T(8,128)(2,1)} %pad_maximum_fusion.3), channel_id=1, source_target_pairs={{0,4},{4,8},{8,12},{1,5},{5,9},{9,13},{2,6},{6,10},{10,14},{3,7},{... | collective-permute-start | bytes 37748744 | tf_op jit(solution)/shard_map/ppermute | solution.py:15
  815.4 7.7 slice-start
  815.4 7.7 slice-start.1
  864.1 5.1 slice-start.2
  864.1 5.1 copy-start.3
  864.1 5.1 slice-start.3
  1136.3 9.5 copy-start.6
  1136.3 9.5 copy-start.7
  1136.3 9.5 copy-start.1
  1136.3 9.5 copy-start.2
  1136.3 9.7 copy-start
where the time goes:
time: 1170 us; the launch traced here: 1160 us
  waiting for transfers between devices  485 us (41%)
  matrix products  201 us (17%)
  local copies, waits for them, and re-layouts  159 us (14%)
  other arithmetic  156 us (13%)
  blocking collectives  137 us (12%)
  starting transfers between devices  14.5 us (1%)
    all_to_all x1, waiting for transfers between devices, per_device(): lax.all_to_all(volt, 'inp', split_axis=1, concat_axis=3, tiled=True)  485 us
    all_gather x3, blocking collectives, carried_in(): pieces = jax.tree.map(lambda part: lax.all_gather(part, axis), value)  137 us
    dot_general x8, matrix products, level_block(): jnp.einsum('cbu,btu->cbt', power_part, kernel, precision=lax.Precision.HI...  74.6 us
    convert_element_type x1, other arithmetic, dedisperse(): (imag_part * chirp_cos - real_part * chirp_sin).reshape(-1, extent)  56.9 us
    another operation x4, other arithmetic  49.1 us
    unnamed x44, local copies, waits for them, and re-layouts  47 us
    dot_general x2, matrix products, per_device(): jnp.einsum('cbrs,csl->cbrl', station_weights, flattened, preferred_elemen...  38.1 us
    dot_general x2, matrix products, dedisperse(): jnp.dot(rows_cur, forward_cur, preferred_element_type=jnp.float32)  36.8 us
  transfers between devices with their start and end apart: 2, of which 1 were waited for; matrix products, arithmetic and copies ran while one was open for 9% of the time, Pallas kernels for 0%

commit v1 on v0

v1 whole, which is shorter than its diff:
```python
import functools
import math

import jax
import jax.numpy as jnp
import ml_dtypes
import numpy as np
from jax import lax
from jax.experimental import pallas as pl
from jax.experimental.pallas import tpu as pltpu
from jax.sharding import PartitionSpec as P

C = 96
NDM = 32
MESH = pl.DeviceIdType.MESH
WINDOW = 4
SLOTS = 4
LANES = 128


def transform_tables(length):
    extent = 2 * length
    indices = np.arange(extent, dtype=np.int64)
    angle = (indices[:, None] * indices[None, :] % extent) * (math.pi / length)
    cosine = np.cos(angle)
    sine = np.sin(angle)
    forward = np.block([[cosine, -sine], [sine, cosine]])
    inverse = np.block([[cosine[:, length:], sine[:, length:]], [-sine[:, length:], cosine[:, length:]]])
    narrow = lambda table: table.astype(np.float32).astype(ml_dtypes.bfloat16)
    return narrow(forward), narrow(inverse)


def cos_sin(x):
    turns = jnp.floor(x * (2.0 / math.pi) + 0.5)
    r = x - turns * 1.5703125
    r = r - turns * 4.837512969970703125e-4
    r = r - turns * 7.549789948768648e-8
    quarter = turns.astype(jnp.int32)
    z = r * r
    s = r + r * z * (-1.6666654611e-1 + z * (8.3321608736e-3 + z * -1.9515295891e-4))
    c = 1.0 - 0.5 * z + z * z * (4.166664568298827e-2 + z * (-1.388731625493765e-3 + z * 2.443315711809948e-5))
    swap = (quarter & 1) == 1
    cosine = jnp.where(swap, s, c)
    sine = jnp.where(swap, c, s)
    cosine = jnp.where(((quarter + 1) & 2) == 2, -cosine, cosine)
    sine = jnp.where((quarter & 2) == 2, -sine, sine)
    return cosine, sine


def kernel(
    n_inp, n_blk,
    volt, gains, positions, columns, pattern, retention, forward_hbm, inverse_hbm,
    partial, correction, entry,
    samples, previous, current, weights, delay, mask, chirp, turned, keep, inv_weight, cum,
    forward, inverse, out_buf, totals, decays,
    volt_send, volt_recv, own_sem, beam_send, beam_recv, out_sem, table_sem,
    total_send, total_recv, decay_send, decay_recv,
):
    here = gains.shape[1]
    stations = positions.shape[1]
    share = volt.shape[3]
    beams, length = retention.shape
    extent = 2 * length
    steps = keep.shape[0]
    z = lax.axis_index("inp")
    t = lax.axis_index("tblk")

    barrier = pltpu.get_barrier_semaphore()
    for s in range(1, n_inp):
        pl.semaphore_signal(barrier, inc=1, device_id={"inp": lax.rem(z + s, n_inp)}, device_id_type=MESH)
    for s in range(1, n_blk):
        pl.semaphore_signal(barrier, inc=1, device_id={"tblk": lax.rem(t + s, n_blk)}, device_id_type=MESH)
    pl.semaphore_wait(barrier, n_inp - 1 + n_blk - 1)

    def rows_of(device):
        return pl.ds(pl.multiple_of(device * share, share), share)

    def volt_out(j, s):
        to = lax.rem(z + s, n_inp)
        return pltpu.make_async_remote_copy(
            src_ref=volt.at[:, to * here + j],
            dst_ref=samples.at[j, :, :, rows_of(z)],
            send_sem=volt_send.at[j, s],
            recv_sem=volt_recv.at[j, s],
            device_id={"inp": to},
            device_id_type=MESH,
        )

    def volt_in(j, s):
        source = lax.rem(z + n_inp - s, n_inp)
        return pltpu.make_async_remote_copy(
            src_ref=volt.at[:, source * here + j],
            dst_ref=samples.at[j, :, :, rows_of(source)],
            send_sem=volt_send.at[j, s],
            recv_sem=volt_recv.at[j, s],
            device_id={"inp": source},
            device_id_type=MESH,
        )

    def volt_own(j):
        return pltpu.make_async_copy(volt.at[:, z * here + j], samples.at[j, :, :, rows_of(z)], own_sem.at[j])

    def beams_out(j):
        slot = lax.rem(j, SLOTS)
        return pltpu.make_async_remote_copy(
            src_ref=current.at[slot],
            dst_ref=previous.at[j],
            send_sem=beam_send.at[slot],
            recv_sem=beam_recv.at[j],
            device_id={"tblk": lax.rem(t + 1, n_blk)},
            device_id_type=MESH,
        )

    def result_out(j):
        slot = lax.rem(j, 2)
        return pltpu.make_async_copy(out_buf.at[slot], partial.at[j], out_sem.at[slot])

    def to_blocks(buffer, s, send, recv, source):
        return pltpu.make_async_remote_copy(
            src_ref=buffer.at[source],
            dst_ref=buffer.at[source],
            send_sem=send.at[s],
            recv_sem=recv.at[s],
            device_id={"tblk": lax.rem(t + s, n_blk)},
            device_id_type=MESH,
        )

    def send_channel(j):
        for s in range(1, n_inp):
            volt_out(j, s).start()
        volt_own(j).start()

    for j in range(min(WINDOW, here)):
        send_channel(j)

    tables = [
        pltpu.make_async_copy(forward_hbm, forward, table_sem.at[0]),
        pltpu.make_async_copy(inverse_hbm, inverse, table_sem.at[1]),
    ]
    for table in tables:
        table.start()

    delay[...] = (
        columns[:, 0:1] * positions[0:1, :]
        + columns[:, 1:2] * positions[1:2, :]
        + columns[:, 2:3] * positions[2:3, :]
    )
    groups, blocks = pattern.shape
    rise = lax.broadcasted_iota(jnp.int32, (beams, groups), 0) // (beams // groups)
    rise = (rise == lax.broadcasted_iota(jnp.int32, (beams, groups), 1)).astype(jnp.float32).astype(jnp.bfloat16)
    wide = lax.broadcasted_iota(jnp.int32, (blocks, stations), 1) // (stations // blocks)
    wide = (wide == lax.broadcasted_iota(jnp.int32, (blocks, stations), 0)).astype(jnp.float32).astype(jnp.bfloat16)
    cells = pattern[...].astype(jnp.float32).astype(jnp.bfloat16)
    spread = jnp.dot(rise, cells, preferred_element_type=jnp.float32).astype(jnp.bfloat16)
    mask[...] = jnp.dot(spread, wide, preferred_element_type=jnp.float32)

    moment = lax.broadcasted_iota(jnp.int32, (beams, length), 1)
    cum[...] = retention[...]
    inv_weight[...] = 1.0 - retention[...]
    for k in range(steps):
        reach = 1 << k
        product = cum[...]
        masked = jnp.where(moment >= reach, product, 0.0)
        keep[k] = masked
        inv_weight[...] += masked * pltpu.roll(inv_weight[...], reach, 1)
        cum[...] = product * jnp.where(moment >= reach, pltpu.roll(product, reach, 1), 1.0)
    lane = lax.broadcasted_iota(jnp.int32, (beams, LANES), 1)
    decays[t] = jnp.where(
        lane == 0,
        cum[:, length - 1 : length],
        inv_weight[:, length - 1 : length],
    )
    for s in range(1, n_blk):
        to_blocks(decays, s, decay_send, decay_recv, t).start()
    for s in range(1, n_blk):
        to_blocks(decays, s, decay_send, decay_recv, t).wait_send()
        to_blocks(decays, s, decay_send, decay_recv, lax.rem(t + n_blk - s, n_blk)).wait_recv()
    carried = jnp.zeros((beams, 1), jnp.float32)
    for i in range(n_blk - 1):
        longer = decays[i, :, 0:1] * carried + decays[i, :, 1:2]
        carried = jnp.where(i < t, longer, carried)
    inv_weight[...] = 1.0 / (inv_weight[...] + cum[...] * carried)
    correction[...] = cum[...] * inv_weight[...]
    totals[t] = jnp.zeros((beams, LANES), jnp.float32)
    for table in tables:
        table.wait()

    tile = 32

    def frequency_of(j, width):
        channel = lax.broadcasted_iota(jnp.int32, (1, width), 1) * 0 + (z * here + j)
        return 1.0 + channel.astype(jnp.float32) / C

    def make_weights(j):
        turning = (2.0 * math.pi) * frequency_of(j, stations)
        gain_real = gains[0, pl.ds(j, 1), :]
        gain_imag = gains[1, pl.ds(j, 1), :]

        @pl.loop(0, beams // tile)
        def _(i):
            rows = pl.ds(pl.multiple_of(i * tile, tile), tile)
            lower = pl.ds(pl.multiple_of(beams + i * tile, tile), tile)
            cosine, sine = cos_sin(turning * delay[rows, :])
            open_here = mask[rows, :]
            real = open_here * (gain_real * cosine + gain_imag * sine)
            imag = open_here * (gain_imag * cosine - gain_real * sine)
            weights[rows, 0:stations] = real.astype(jnp.bfloat16)
            weights[rows, stations:] = (-imag).astype(jnp.bfloat16)
            weights[lower, 0:stations] = imag.astype(jnp.bfloat16)
            weights[lower, stations:] = real.astype(jnp.bfloat16)

    def make_chirp(j):
        frequency = frequency_of(j, extent)
        index = lax.broadcasted_iota(jnp.int32, (1, extent), 1)
        offsets = jnp.where(index < length, index, index - extent).astype(jnp.float32) / extent
        shape = offsets * offsets / (frequency * frequency * frequency)

        @pl.loop(0, beams // tile)
        def _(i):
            rows = pl.ds(pl.multiple_of(i * tile, tile), tile)
            cosine, sine = cos_sin((math.pi * length) * columns[rows, 3:4] * shape)
            chirp[0, rows, :] = cosine
            chirp[1, rows, :] = sine

    @pl.loop(0, here + 1)
    def _(step):
        @pl.when(step < here)
        def _():
            j = step
            make_weights(j)
            for s in range(1, n_inp):
                volt_in(j, s).wait_recv()
            volt_own(j).wait()
            for s in range(1, n_inp):
                volt_out(j, s).wait_send()

            @pl.when(j + WINDOW < here)
            def _():
                send_channel(j + WINDOW)

            @pl.when(j >= SLOTS)
            def _():
                beams_out(j - SLOTS).wait_send()

            slot = lax.rem(j, SLOTS)
            for p in range(2):
                formed = jnp.dot(
                    weights[...],
                    samples[j, p].reshape(2 * stations, length),
                    preferred_element_type=jnp.float32,
                ).astype(jnp.bfloat16)
                current[slot, 0, p * beams : (p + 1) * beams] = formed[:beams]
                current[slot, 1, p * beams : (p + 1) * beams] = formed[beams:]
            beams_out(j).start()

        @pl.when(step >= 1)
        def _():
            j = step - 1
            make_chirp(j)
            beams_out(j).wait_recv()
            slot = lax.rem(j, SLOTS)
            first = t == 0
            power = jnp.zeros((beams, length), jnp.float32)
            for p in range(2):
                part = slice(p * beams, (p + 1) * beams)
                behind_real = previous[j, 0, part]
                behind_imag = previous[j, 1, part]
                nothing = jnp.zeros_like(behind_real)
                series = jnp.concatenate(
                    [
                        jnp.where(first, nothing, behind_real),
                        current[slot, 0, part],
                        jnp.where(first, nothing, behind_imag),
                        current[slot, 1, part],
                    ],
                    axis=1,
                )
                for k in range(2):
                    low, high = k * length, (k + 1) * length
                    real = jnp.dot(series, forward[:, low:high], preferred_element_type=jnp.float32)
                    imag = jnp.dot(
                        series, forward[:, extent + low : extent + high], preferred_element_type=jnp.float32
                    )
                    cosine = chirp[0, :, low:high]
                    sine = chirp[1, :, low:high]
                    turned[:, low:high] = (real * cosine + imag * sine).astype(jnp.bfloat16)
                    turned[:, extent + low : extent + high] = (imag * cosine - real * sine).astype(jnp.bfloat16)
                for half in range(2):
                    signal = jnp.dot(
                        turned[...],
                        inverse[:, half * length : (half + 1) * length],
                        preferred_element_type=jnp.float32,
                    ) * (1.0 / extent)
                    power += signal * signal

            level = (1.0 - retention[...]) * power
            for k in range(steps):
                level += keep[k] * pltpu.roll(level, 1 << k, 1)
            totals[t] = jnp.where(lane == j, level[:, length - 1 : length], totals[t])

            @pl.when(j >= 2)
            def _():
                result_out(j - 2).wait()

            out_buf[lax.rem(j, 2)] = power - level * inv_weight[...]
            result_out(j).start()

    for s in range(1, n_blk):
        to_blocks(totals, s, total_send, total_recv, t).start()
    for j in range(max(here - SLOTS, 0), here):
        beams_out(j).wait_send()
    for j in range(max(here - 2, 0), here):
        result_out(j).wait()
    for s in range(1, n_blk):
        to_blocks(totals, s, total_send, total_recv, t).wait_send()
        to_blocks(totals, s, total_send, total_recv, lax.rem(t + n_blk - s, n_blk)).wait_recv()
    carried = jnp.zeros((beams, LANES), jnp.float32)
    for i in range(n_blk - 1):
        longer = decays[i, :, 0:1] * carried + totals[i]
        carried = jnp.where(i < t, longer, carried)
    entry[...] = carried


def per_device(volt, gains, positions, directions, pattern, dm_bins, retention):
    n_inp, n_blk = lax.axis_size("inp"), lax.axis_size("tblk")
    here = gains.shape[1]
    stations = positions.shape[1]
    beams, length = retention.shape
    extent = 2 * length
    steps = (length - 1).bit_length()
    measure = (dm_bins + 1).astype(jnp.float32) / NDM
    columns = jnp.concatenate([directions, measure[None, :]], axis=0).T
    forward, inverse = transform_tables(length)
    inside = pl.BlockSpec(memory_space=pltpu.VMEM)
    outside = pl.BlockSpec(memory_space=pl.ANY)
    f32, bf16 = jnp.float32, jnp.bfloat16
    dma = pltpu.SemaphoreType.DMA
    partial, correction, entry = pl.pallas_call(
        functools.partial(kernel, n_inp, n_blk),
        out_shape=[
            jax.ShapeDtypeStruct((here, beams, length), f32),
            jax.ShapeDtypeStruct((beams, length), f32),
            jax.ShapeDtypeStruct((beams, LANES), f32),
        ],
        in_specs=[outside, inside, inside, inside, inside, inside, outside, outside],
        out_specs=[outside, inside, inside],
        scratch_shapes=[
            pltpu.VMEM((here, 2, 2, stations, length), bf16),
            pltpu.VMEM((here, 2, 2 * beams, length), bf16),
            pltpu.VMEM((SLOTS, 2, 2 * beams, length), bf16),
            pltpu.VMEM((2 * beams, 2 * stations), bf16),
            pltpu.VMEM((beams, stations), f32),
            pltpu.VMEM((beams, stations), f32),
            pltpu.VMEM((2, beams, extent), f32),
            pltpu.VMEM((beams, 2 * extent), bf16),
            pltpu.VMEM((steps, beams, length), f32),
            pltpu.VMEM((beams, length), f32),
            pltpu.VMEM((beams, length), f32),
            pltpu.VMEM((2 * extent, 2 * extent), bf16),
            pltpu.VMEM((2 * extent, extent), bf16),
            pltpu.VMEM((2, beams, length), f32),
            pltpu.VMEM((n_blk, beams, LANES), f32),
            pltpu.VMEM((n_blk, beams, LANES), f32),
            dma((here, n_inp)),
            dma((here, n_inp)),
            dma((here,)),
            dma((SLOTS,)),
            dma((here,)),
            dma((2,)),
            dma((2,)),
            dma((n_blk,)),
            dma((n_blk,)),
            dma((n_blk,)),
            dma((n_blk,)),
        ],
        compiler_params=pltpu.CompilerParams(
            collective_id=0, has_side_effects=True, vmem_limit_bytes=60 * 1024 * 1024
        ),
        cost_estimate=pl.CostEstimate(
            flops=2 * here * 2 * beams * (2 * stations * 2 * length + 2 * extent * 3 * extent),
            bytes_accessed=2 * volt.size + 4 * here * beams * length,
            transcendentals=0,
        ),
    )(volt, gains, positions, columns, pattern, retention, jnp.asarray(forward), jnp.asarray(inverse))
    late = correction[None] * entry[:, :here].T[:, :, None]
    return jnp.transpose(partial - late, (1, 0, 2))


def solution(mesh):
    placed = (
        P(None, "grp", None, "inp", "tblk"),
        P(None, ("grp", "inp"), None),
        P(),
        P(),
        P(),
        P(),
        P(None, "tblk"),
    )
    return jax.shard_map(
        per_device,
        mesh=mesh,
        in_specs=placed,
        out_specs=P(None, ("grp", "inp"), "tblk"),
        check_vma=False,
    )
```

time: 1170 us -> 578 us (0.49)
  Pallas kernels: 0 us -> 560 us
  waiting for transfers between devices: 485 us -> 0 us
  matrix products: 201 us -> 0 us
  other arithmetic: 156 us -> 4.8 us
  local copies, waits for them, and re-layouts: 159 us -> 8.12 us
  blocking collectives: 137 us -> 0 us
  starting transfers between devices: 14.5 us -> 0 us
    pallas_call x0 -> x1, Pallas kernels: none -> 560 us  [per_device(): pl.pallas_call(functools.partial(kernel, n_inp, n_blk), out_shape=[jax.Sh...]
    all_to_all x1 -> x0, waiting for transfers between devices: 485 us -> none  [per_device(): lax.all_to_all(volt, 'inp', split_axis=1, concat_axis=3, tiled=True)]
    dot_general x18 -> x0, matrix products: 201 us -> none  [the longest x8 74.6 us: level_block(): jnp.einsum('cbu,btu->cbt', power_part, kernel, precision=lax.Precision.HI...]
    all_gather x3 -> x0, blocking collectives: 137 us -> none  [carried_in(): pieces = jax.tree.map(lambda part: lax.all_gather(part, axis), value)]
    another operation x6 -> x0, other arithmetic: 69.1 us -> none
    convert_element_type x3 -> x0, other arithmetic: 61.2 us -> none  [the longest x1 56.9 us: dedisperse(): (imag_part * chirp_cos - real_part * chirp_sin).reshape(-1, extent)]
    unnamed x44 -> x0, local copies, waits for them, and re-layouts: 47 us -> none
    slice x11 -> x0, local copies, waits for them, and re-layouts: 41.6 us -> none  [the longest x3 28.7 us: dedisperse(): rows_prev = previous[polar].reshape(-1, extent)]
  transfers between devices with their start and end apart: 2 -> 0, of which waited for: 1 -> 0; matrix products, arithmetic and copies ran while one was open for 9% -> 0% of each run, Pallas kernels for 0% -> 0%
where the time goes in v1:
time: 578 us; the launch traced here: 573 us
  Pallas kernels  560 us (97%)
  local copies, waits for them, and re-layouts  8.12 us (1%)
    pallas_call x1, Pallas kernels, per_device(): pl.pallas_call(functools.partial(kernel, n_inp, n_blk), out_shape=[jax.Sh...  560 us

profile of v1, /device:TPU:0, one launch (start us, length us, event | category | flops | bytes accessed | tf_op | source)
XLA Modules:
  0.0 573.1 jit_solution(5632437238247177456)
XLA Ops:
  0.0 0.7 convert_multiply_fusion
  0.7 0.7 pad_maximum_fusion
  1.4 0.8 copy.17
  2.2 560.2 %shard_map.91 = (f32[24,256,256]{2,1,0:T(8,128)}, f32[256,256]{1,0:T(8,128)}, f32[256,128]{1,0:T(8,128)}) custom-call(bf16[2,96,2,128,256]{4,3,2,1,0:T(8,128)(2,1)} %volt.1, f32[2,24,512]{2,1,0:T(8,128)} %gains.1, f32[3,512]{1,0:T(4,128)} %positions.1, f32[256,4]{1,0:T(8,128)} %bitcast.6, s32[32,64]{1,0:T(8,128)} %pattern.1, f32[256,256]{1,0:T(8,128)} %retention.1, ...), custom_call_target="tpu_custom_call" | custom-call | flops 51539607552 | bytes 31457280 | tf_op jit(solution)/shard_map/pallas_call | solution.py:338
  562.3 0.9 slice_bitcast_fusion
  563.3 0.1 copy.18
  563.3 3.4 subtract_bitcast_fusion
  566.8 6.3 %copy.19 = f32[256,24,256]{2,1,0:T(8,128)} copy(f32[256,24,256]{2,0,1:T(8,128)S(1)} %subtract_bitcast_fusion) | data formatting | bytes 12582912 | tf_op jit(solution)/shard_map/transpose | solution.py:386

commit v2 on v1

--- a/solution.py
+++ b/solution.py
@@ -52,7 +52,7 @@
     volt, gains, positions, columns, pattern, retention, forward_hbm, inverse_hbm,
     partial, correction, entry,
     samples, previous, current, weights, delay, mask, chirp, turned, keep, inv_weight, cum,
-    forward, inverse, out_buf, totals, decays,
+    forward, inverse, out_buf, ends, totals, decays, decay_rows,
     volt_send, volt_recv, own_sem, beam_send, beam_recv, out_sem, table_sem,
     total_send, total_recv, decay_send, decay_recv,
 ):
@@ -62,6 +62,8 @@
     beams, length = retention.shape
     extent = 2 * length
     steps = keep.shape[0]
+    bunch = out_buf.shape[2]
+    held = totals.shape[1]
     z = lax.axis_index("inp")
     t = lax.axis_index("tblk")
 
@@ -112,8 +114,13 @@
         )
 
     def result_out(j):
-        slot = lax.rem(j, 2)
-        return pltpu.make_async_copy(out_buf.at[slot], partial.at[j], out_sem.at[slot])
+        group = j // bunch
+        slot = lax.rem(group, 2)
+        return pltpu.make_async_copy(
+            out_buf.at[slot],
+            partial.at[:, pl.ds(pl.multiple_of(group * bunch, bunch), bunch)],
+            out_sem.at[slot],
+        )
 
     def to_blocks(buffer, s, send, recv, source):
         return pltpu.make_async_remote_copy(
@@ -181,7 +188,9 @@
         carried = jnp.where(i < t, longer, carried)
     inv_weight[...] = 1.0 / (inv_weight[...] + cum[...] * carried)
     correction[...] = cum[...] * inv_weight[...]
-    totals[t] = jnp.zeros((beams, LANES), jnp.float32)
+    ends[...] = jnp.zeros((beams, LANES), jnp.float32)
+    for i in range(n_blk - 1):
+        decay_rows[i] = jnp.transpose(decays[i])[0:8]
     for table in tables:
         table.wait()
 
@@ -296,27 +305,31 @@
             level = (1.0 - retention[...]) * power
             for k in range(steps):
                 level += keep[k] * pltpu.roll(level, 1 << k, 1)
-            totals[t] = jnp.where(lane == j, level[:, length - 1 : length], totals[t])
-
-            @pl.when(j >= 2)
+            ends[...] = jnp.where(lane == j, level[:, length - 1 : length], ends[...])
+
+            @pl.when((lax.rem(j, bunch) == 0) & (j >= 2 * bunch))
             def _():
-                result_out(j - 2).wait()
-
-            out_buf[lax.rem(j, 2)] = power - level * inv_weight[...]
-            result_out(j).start()
-
+                result_out(j - 2 * bunch).wait()
+
+            out_buf[lax.rem(j // bunch, 2), :, lax.rem(j, bunch), :] = power - level * inv_weight[...]
+
+            @pl.when(lax.rem(j, bunch) == bunch - 1)
+            def _():
+                result_out(j).start()
+
+    totals[t] = jnp.transpose(ends[...])[0:held]
     for s in range(1, n_blk):
         to_blocks(totals, s, total_send, total_recv, t).start()
     for j in range(max(here - SLOTS, 0), here):
         beams_out(j).wait_send()
-    for j in range(max(here - 2, 0), here):
-        result_out(j).wait()
+    for group in range(max(here // bunch - 2, 0), here // bunch):
+        result_out(group * bunch).wait()
     for s in range(1, n_blk):
         to_blocks(totals, s, total_send, total_recv, t).wait_send()
         to_blocks(totals, s, total_send, total_recv, lax.rem(t + n_blk - s, n_blk)).wait_recv()
-    carried = jnp.zeros((beams, LANES), jnp.float32)
+    carried = jnp.zeros((held, beams), jnp.float32)
     for i in range(n_blk - 1):
-        longer = decays[i, :, 0:1] * carried + totals[i]
+        longer = decay_rows[i, 0:1, :] * carried + totals[i]
         carried = jnp.where(i < t, longer, carried)
     entry[...] = carried
 
@@ -328,6 +341,8 @@
     beams, length = retention.shape
     extent = 2 * length
     steps = (length - 1).bit_length()
+    bunch = 8 if here % 8 == 0 else here
+    held = -(-here // 8) * 8
     measure = (dm_bins + 1).astype(jnp.float32) / NDM
     columns = jnp.concatenate([directions, measure[None, :]], axis=0).T
     forward, inverse = transform_tables(length)
@@ -338,9 +353,9 @@
     partial, correction, entry = pl.pallas_call(
         functools.partial(kernel, n_inp, n_blk),
         out_shape=[
-            jax.ShapeDtypeStruct((here, beams, length), f32),
+            jax.ShapeDtypeStruct((beams, here, length), f32),
             jax.ShapeDtypeStruct((beams, length), f32),
-            jax.ShapeDtypeStruct((beams, LANES), f32),
+            jax.ShapeDtypeStruct((held, beams), f32),
         ],
         in_specs=[outside, inside, inside, inside, inside, inside, outside, outside],
         out_specs=[outside, inside, inside],
@@ -358,9 +373,11 @@
             pltpu.VMEM((beams, length), f32),
             pltpu.VMEM((2 * extent, 2 * extent), bf16),
             pltpu.VMEM((2 * extent, extent), bf16),
-            pltpu.VMEM((2, beams, length), f32),
+            pltpu.VMEM((2, beams, bunch, length), f32),
+            pltpu.VMEM((beams, LANES), f32),
+            pltpu.VMEM((n_blk, held, beams), f32),
             pltpu.VMEM((n_blk, beams, LANES), f32),
-            pltpu.VMEM((n_blk, beams, LANES), f32),
+            pltpu.VMEM((n_blk, 8, beams), f32),
             dma((here, n_inp)),
             dma((here, n_inp)),
             dma((here,)),
@@ -382,8 +399,7 @@
             transcendentals=0,
         ),
     )(volt, gains, positions, columns, pattern, retention, jnp.asarray(forward), jnp.asarray(inverse))
-    late = correction[None] * entry[:, :here].T[:, :, None]
-    return jnp.transpose(partial - late, (1, 0, 2))
+    return partial - correction[:, None, :] * entry[:here].T[:, :, None]
 
 
 def solution(mesh):

time: 578 us -> 570 us (0.986)
  local copies, waits for them, and re-layouts: 8.12 us -> 1.64 us
    transpose x3 -> x1, local copies, waits for them, and re-layouts: 7.32 us -> 0.84 us  [per_device(): return partial - correction[:, None, :] * entry[:here].T[:, :, None]]
where the time goes in v2:
time: 570 us; the launch traced here: 567 us
  Pallas kernels  559 us (98%)
  other arithmetic  6.45 us (1%)
    pallas_call x1, Pallas kernels, per_device(): pl.pallas_call(functools.partial(kernel, n_inp, n_blk), out_shape=[jax.Sh...  559 us

profile of v2, /device:TPU:0, one launch (start us, length us, event | category | flops | bytes accessed | tf_op | source)
XLA Modules:
  0.0 566.8 jit_solution(7912491666350343021)
XLA Ops:
  0.0 0.7 convert_multiply_fusion
  0.7 0.7 pad_maximum_fusion
  1.4 0.8 copy.15
  2.2 558.7 %shard_map.91 = (f32[256,24,256]{2,1,0:T(8,128)}, f32[256,256]{1,0:T(8,128)}, f32[24,256]{1,0:T(8,128)}) custom-call(bf16[2,96,2,128,256]{4,3,2,1,0:T(8,128)(2,1)} %volt.1, f32[2,24,512]{2,1,0:T(8,128)} %gains.1, f32[3,512]{1,0:T(4,128)} %positions.1, f32[256,4]{1,0:T(8,128)} %bitcast.3, s32[32,64]{1,0:T(8,128)} %pattern.1, f32[256,256]{1,0:T(8,128)} %retention.1, ...), custom_call_target="tpu_custom_call" | custom-call | flops 51539607552 | bytes 31457280 | tf_op jit(solution)/shard_map/pallas_call | solution.py:353
  560.9 0.8 copy.16
  561.7 5.1 multiply_subtract_fusion
